TPU v7x, 32 devices: a whole 2x2x4 slice. The times are simulated.
32 devices in a mesh: groups: 2 (over x), rows: 16 (over z, y, core).
Axes of the slice: x: 2, y: 2, z: 4, core: 2. Of those that a mesh axis runs over, the one named last changes fastest.
Arguments:
- features: bfloat16 [16384, 128], P(('groups', 'rows')), parts along dimension 0, may hold values from -6 to 6
- block_cols: int32 [1024], P(('groups', 'rows')), parts along dimension 0, may hold values from 0 to 63, as said below
- block_vals: bfloat16 [1024, 128, 128], P(('groups', 'rows')), parts along dimension 0, may hold values from 0 to 1, as said below
- degree: int32 [16384], P(('groups', 'rows')), parts along dimension 0, may hold values from 1 to 1040, as said below
- w_self: bfloat16 [128, 256], replicated, may hold values from -0.5 to 0.5
- w_neigh: bfloat16 [128, 256], replicated, may hold values from -0.5 to 0.5
- cotangent: bfloat16 [16384, 256], P(('groups', 'rows')), parts along dimension 0, may hold values from -6 to 6
Outputs:
- output: bfloat16 [16384, 256], P(('groups', 'rows')), parts along dimension 0
- grad_features: bfloat16 [16384, 128], P(('groups', 'rows')), parts along dimension 0
- grad_self: float32 [256, 256], P('groups'), parts along dimension 0
- grad_neigh: float32 [256, 256], P('groups'), parts along dimension 0
There are 2 independent parts, one for each index of `groups`. A program takes and returns all parts, laid end to end along the dimension named above; an argument that names none is the same for every part. Nothing has to cross between parts.
Inputs may be any that keep to these rules, and one draw needn't show every extreme that they name: `block_cols`: the 32 entries of one device name blocks of exactly 16 owners (the owner of block c holds nodes of blocks c - c % 4 to c - c % 4 + 3), each of these owners named by exactly 2 of that device's entries; a block may be named twice. `block_vals`: each entry is 0 or 1. A node's degree is its row sum of A plus its neighbours outside the batch: 1 to 16 of them for every node but the batch's first two; the second node has no neighbour in the batch and one outside, and the first has degree exactly 1040.
All inputs are finite; a program needn't handle non-finite values.
Results may differ from a plain program's by a relative error of at most 0.0052.
Values may be sent and summed in bfloat16 or wider, within the bound.
A program may use at most 64 MiB of HBM per device.

v0:
```python
import jax
import jax.numpy as jnp
from jax import lax
from jax.sharding import PartitionSpec as P


def body(features, block_cols, block_vals, degree, w_self, w_neigh, cotangent):
    nodes_dev, width = features.shape
    row_blocks = nodes_dev // 128
    per_row = block_cols.shape[0] // row_blocks
    devices = lax.axis_size("rows")
    everything = lax.all_gather(features, "rows", axis=0, tiled=True)
    neighbour = everything.reshape(-1, 128, width)[block_cols]
    terms = jnp.einsum("bij,bjf->bif", block_vals, neighbour, preferred_element_type=jnp.float32)
    aggregate = terms.reshape(row_blocks, per_row, 128, width).sum(1).reshape(nodes_dev, width)
    scale = degree.astype(jnp.float32)[:, None]
    mean = (aggregate / scale).astype(jnp.bfloat16)
    pre = jnp.dot(features, w_self, preferred_element_type=jnp.float32) + jnp.dot(
        mean, w_neigh, preferred_element_type=jnp.float32
    )
    sigma = jax.nn.sigmoid(pre)
    output = (pre * sigma).astype(jnp.bfloat16)
    dpre = (cotangent.astype(jnp.float32) * sigma * (1.0 + pre * (1.0 - sigma))).astype(
        jnp.bfloat16
    )
    sums = lax.psum(
        (
            jnp.dot(features.T, dpre, preferred_element_type=jnp.float32),
            jnp.dot(mean.T, dpre, preferred_element_type=jnp.float32),
        ),
        "rows",
    )
    factor = float(nodes_dev * devices) ** (-0.5)
    dagg = (jnp.dot(dpre, w_neigh.T, preferred_element_type=jnp.float32) / scale).astype(
        jnp.bfloat16
    )
    dagg_blocks = jnp.repeat(dagg.reshape(row_blocks, 128, width), per_row, axis=0)
    back = jnp.einsum("bji,bjf->bif", block_vals, dagg_blocks, preferred_element_type=jnp.float32)
    count = nodes_dev * lax.axis_size("rows")
    number = count // 128
    target = block_cols
    target = jnp.where((target >= 0) & (target < number), target, number)
    total = jnp.zeros((number, 128, width), jnp.float32).at[target].add(back, mode="drop")
    spread = lax.psum_scatter(total.reshape(count, width), "rows", scatter_dimension=0, tiled=True)
    grad_features = (jnp.dot(dpre, w_self.T, preferred_element_type=jnp.float32) + spread).astype(
        jnp.bfloat16
    )
    return (output, grad_features, sums[0] * factor, sums[1] * factor)


def solution(mesh):
    return jax.shard_map(
        body,
        mesh=mesh,
        in_specs=(
            P(("groups", "rows"), None),
            P(("groups", "rows")),
            P(("groups", "rows"), None, None),
            P(("groups", "rows")),
            P(),
            P(),
            P(("groups", "rows"), None),
        ),
        out_specs=(
            P(("groups", "rows"), None),
            P(("groups", "rows"), None),
            P("groups", None),
            P("groups", None),
        ),
        check_vma=False,
    )
```

profile of v0, /device:TPU:0, one launch (start us, length us, event | category | flops | bytes accessed | tf_op | source)
XLA Modules:
  0.0 234.6 jit_solution(17850112241904582061)
XLA Ops:
  7.2 0.0 copy-start
  7.2 0.0 all-gather.2.cloned.1.call-start
  7.2 0.7 all-gather.2.cloned.1.call-update
  7.9 0.0 all-reduce.3.cloned.1.call-start
  8.0 0.7 convert_element_type.21
  8.6 0.7 compare_select_fusion
  9.3 1.1 fusion.3
  10.4 43.9 %all-gather.2.cloned.1.call-done = bf16[8192,128]{1,0:T(8,128)(2,1)} async-done(((bf16[512,128]{1,0:T(8,128)(2,1)}), bf16[8192,128]{1,0:T(8,128)(2,1)}) %all-gather.2.cloned.1.call-update) | async-done | bytes 2097168 | tf_op jit(solution)/shard_map/all_gather | solution.py:12
  54.3 2.3 gather_fusion
  56.7 0.0 copy-done
  56.7 0.0 copy-start.3
  56.7 0.0 copy-start.4
  56.7 0.9 bitcast_reduce_fusion
  57.6 0.1 copy.23
  57.7 0.1 fusion.2
  57.8 0.0 copy-done.3
  57.8 0.0 copy-done.4
  57.9 0.0 copy-start.1
  57.9 1.1 multiply_convert_fusion
  59.0 0.2 fusion.1
  59.2 0.0 copy-done.1
  59.2 0.9 convolution_bitcast_fusion.1
  60.2 0.9 fusion.4
  61.1 0.1 copy.24
  61.2 0.0 all-reduce.3.cloned.1.call-update
  61.3 0.0 reduce-scatter.2.cloned.1.call-start
  61.3 0.2 broadcast_in_dim.18
  61.5 1.8 convolution_bitcast_fusion
  63.3 1.9 copy.25
  65.2 2.5 %broadcast_in_dim.16 = f32[64,128,128]{2,1,0:T(8,128)} broadcast(f32[]{:T(128)} %constant.0.clone.1), dimensions={} | broadcast | bytes 4194308 | tf_op jit(solution)/shard_map/broadcast_in_dim | solution.py:43
  67.7 6.2 %scatter_fusion = f32[64,128,128]{2,1,0:T(8,128)} fusion(f32[64,128,128]{2,1,0:T(8,128)} %broadcast_in_dim.16, s32[32]{0:T(128)S(1)} %get-tuple-element.20, f32[32,128,128]{2,1,0:T(8,128)S(1)} %copy.25), kind=kCustom, calls=%fused_computation.1 | custom fusion | flops 524288 | bytes 6291584 | tf_op jit(solution)/shard_map/scatter-add | solution.py:43
  73.9 0.0 copy-start.2
  73.9 0.0 reduce-scatter.2.cloned.1.call-update
  74.0 75.2 %all-reduce.3.cloned.1.call-done = (f32[128,256]{0,1:T(8,128)}, f32[128,256]{0,1:T(8,128)}) async-done(((f32[128,256]{0,1:T(8,128)}, f32[128,256]{0,1:T(8,128)}), (f32[128,256]{0,1:T(8,128)}, f32[128,256]{0,1:T(8,128)})) %all-reduce.3.cloned.1.call-update) | async-done | bytes 262160 | tf_op jit(solution)/shard_map/psum | solution.py:26
  149.2 1.0 broadcast_multiply_fusion
  150.1 0.8 copy.27
  150.9 0.8 copy.28
  151.7 74.6 %reduce-scatter.2.cloned.1.call-done = f32[512,128]{1,0:T(8,128)} async-done(((f32[8192,128]{1,0:T(8,128)}), f32[512,128]{1,0:T(8,128)}) %reduce-scatter.2.cloned.1.call-update) | async-done | bytes 262160 | tf_op jit(solution)/shard_map/reduce_scatter | solution.py:44
  226.3 0.0 copy-done.2
  226.3 1.8 fusion
  (1 shorter events, 0.0 us)
Async XLA Ops:
  7.2 49.5 %copy-start = (bf16[32,128,128]{2,1,0:T(8,128)(2,1)S(1)}, bf16[32,128,128]{2,1,0:T(8,128)(2,1)}, u32[]{:S(2)}) copy-start(bf16[32,128,128]{2,1,0:T(8,128)(2,1)} %param.9) | copy-start | bytes 3145732
  7.2 47.1 %all-gather.2.cloned.1.call-start = ((), (), s32[]{:S(2)}) async-start(), calls=%async_computation.1 | async-start | bytes 2228224 | tf_op jit(solution)/shard_map/all_gather | solution.py:12
  7.9 141.2 %all-reduce.3.cloned.1.call-start = ((), (), s32[]{:S(2)}) async-start(), calls=%async_computation.3 | async-start | bytes 524288 | tf_op jit(solution)/shard_map/psum | solution.py:26
  56.7 1.2 copy-start.3
  56.7 1.2 copy-start.4
  57.9 1.4 copy-start.1
  61.3 165.0 %reduce-scatter.2.cloned.1.call-start = ((), (), s32[]{:S(2)}) async-start(), calls=%async_computation.2 | async-start | bytes 4456448 | tf_op jit(solution)/shard_map/reduce_scatter | solution.py:44
  73.9 152.3 %copy-start.2 = (bf16[128,256]{1,0:T(8,128)(2,1)S(1)}, bf16[128,256]{1,0:T(8,128)(2,1)}, u32[]{:S(2)}) copy-start(bf16[128,256]{1,0:T(8,128)(2,1)} %param.11) | copy-start | bytes 196612
Sparse Core Ops, SparseCore 0:
  10.2 44.0 all-gather.1
  61.4 87.7 all-reduce.2
  153.0 73.1 reduce-scatter.1
where the time goes:
time: 235 us
  waiting for transfers between devices  194 us (83%)
  between operations  13.9 us (6%)
  matrix products  8.79 us (4%)
  local copies, waits for them, and re-layouts  8.74 us (4%)
  other arithmetic  8.71 us (4%)
    psum x1, waiting for transfers between devices, body(): lax.psum((jnp.dot(features.T, dpre, preferred_element_type=jnp.float32),...  75.2 us
    reduce_scatter x1, waiting for transfers between devices, body(): lax.psum_scatter(total.reshape(count, width), 'rows', scatter_dimension=0...  74.6 us
    all_gather x1, waiting for transfers between devices, body(): everything = lax.all_gather(features, 'rows', axis=0, tiled=True)  43.9 us
    scatter-add x1, other arithmetic, body(): jnp.zeros((number, 128, width), jnp.float32).at[target]  6.23 us
  transfers between devices with their start and end apart: 3, of which 3 were waited for; matrix products, arithmetic and copies ran while one was open for 7% of the time, Pallas kernels for 0%

commit v1 on v0

v1 whole, which is shorter than its diff:
```python
import functools

import jax
import jax.numpy as jnp
from jax import lax
from jax.experimental import pallas as pl
from jax.experimental.pallas import tpu as pltpu
from jax.sharding import PartitionSpec as P

B = 128
F32 = jnp.float32
BF16 = jnp.bfloat16
NT = (((1,), (1,)), ((), ()))


def remote(src, dst, send, recv, device):
    return pltpu.make_async_remote_copy(
        src_ref=src,
        dst_ref=dst,
        send_sem=send,
        recv_sem=recv,
        device_id={"rows": device},
        device_id_type=pl.DeviceIdType.MESH,
    )


class Place:
    def __init__(self, z_size, y_size):
        self.Z, self.Y = z_size, y_size
        me = lax.axis_index("rows")
        self.me = me
        self.c = me % 2
        self.y = (me // 2) % y_size
        self.z = me // (2 * y_size)
        self.has_down = self.z > 0
        self.has_up = self.z < z_size - 1

    def index(self, z, y, c):
        return (z * self.Y + y) * 2 + c

    @property
    def up(self):
        return self.index(jnp.minimum(self.z + 1, self.Z - 1), self.y, self.c)

    @property
    def down(self):
        return self.index(jnp.maximum(self.z - 1, 0), self.y, self.c)

    @property
    def across(self):
        return self.index(self.z, (self.y + 1) % self.Y, self.c)

    @property
    def sibling(self):
        return self.index(self.z, self.y, 1 - self.c)

    def by_distance(self, k):
        if k == 0:
            return [(None, self.z)]
        return [
            (self.z + k < self.Z, jnp.minimum(self.z + k, self.Z - 1)),
            (self.z - k >= 0, jnp.maximum(self.z - k, 0)),
        ]


def when(cond):
    if cond is None:
        return lambda f: f()
    return pl.when(cond)


class Gather:
    def __init__(self, place, first, buf, chunks, send, recv):
        self.p, self.first, self.buf = place, first, buf
        self.chunks, self.send, self.recv = chunks, send, recv
        self.blocks = buf.shape[0] // (2 * place.Z * place.Y)
        self.part = self.blocks // chunks

    def copy(self, kind, z, y, h, device, own=False):
        piece = self.p.index(z, y, self.p.c)
        dst = self.buf.at[pl.ds(piece * self.blocks + h * self.part, self.part)]
        src = dst
        if own and self.first is not None:
            src = self.first.at[pl.ds(h * self.part, self.part)]
        return remote(
            src, dst, self.send.at[kind, z, h], self.recv.at[kind, z, h], device
        )

    def arrived(self, kind, z, y, h, c=None):
        piece = self.p.index(z, y, self.p.c if c is None else c)
        dst = self.buf.at[pl.ds(piece * self.blocks + h * self.part, self.part)]
        remote(
            dst, dst, self.send.at[kind, z, h], self.recv.at[kind, z, h], self.p.sibling
        ).wait_recv()

    def run(self):
        p = self.p
        for h in range(self.chunks):
            pl.when(p.has_up)(lambda: self.copy(0, p.z, p.y, h, p.up, True).start())
            pl.when(p.has_down)(lambda: self.copy(1, p.z, p.y, h, p.down, True).start())
            if p.Y > 1:
                self.copy(2, p.z, p.y, h, p.across, True).start()
        for h in range(self.chunks):
            self.copy(3 + p.y, p.z, p.y, h, p.sibling, True).start()
        yield
        for k in range(1, p.Z + 1):
            for h in range(self.chunks):
                if k < p.Z:
                    for kind, cond, z in (
                        (0, p.z - k >= 0, jnp.maximum(p.z - k, 0)),
                        (1, p.z + k < p.Z, jnp.minimum(p.z + k, p.Z - 1)),
                    ):

                        @pl.when(cond)
                        def _():
                            self.arrived(kind, z, p.y, h)
                            on, target = ((p.has_up, p.up), (p.has_down, p.down))[kind]
                            pl.when(on)(lambda: self.copy(kind, z, p.y, h, target).start())
                            if p.Y > 1:
                                self.copy(2, z, p.y, h, p.across).start()
                            self.copy(3 + p.y, z, p.y, h, p.sibling).start()

                if p.Y > 1:
                    for cond, z in p.by_distance(k - 1):

                        @when(cond)
                        def _():
                            self.arrived(2, z, 1 - p.y, h)
                            self.copy(4 - p.y, z, 1 - p.y, h, p.sibling).start()

            yield
        for z in range(p.Z):
            for y in range(p.Y):
                for h in range(self.chunks):
                    self.arrived(3 + y, z, y, h, 1 - p.c)
        yield

    def finish(self):
        p = self.p
        for z in range(p.Z):
            for h in range(self.chunks):
                pl.when(p.has_up & (z <= p.z))(
                    lambda: self.copy(0, z, p.y, h, p.up).wait_send()
                )
                pl.when(p.has_down & (z >= p.z))(
                    lambda: self.copy(1, z, p.y, h, p.down).wait_send()
                )
                if p.Y > 1:
                    self.copy(2, z, p.y, h, p.across).wait_send()
                for y in range(p.Y):
                    self.copy(3 + y, z, y, h, p.sibling).wait_send()


class Reduce:
    def __init__(self, place, total, from_core, from_y, from_z, chunks, send, recv):
        self.p, self.total = place, total
        self.from_core, self.from_y, self.from_z = from_core, from_y, from_z
        self.chunks, self.send, self.recv = chunks, send, recv
        self.rows = total.shape[1] // chunks

    def copy(self, kind, z, y, c, h, device):
        rows = pl.ds(h * self.rows, self.rows)
        if kind is None:
            kind, dst = 3 + y, self.from_core.at[y, z, rows]
        elif kind == 2:
            dst = self.from_y.at[z, rows]
        else:
            dst = self.from_z.at[kind, z, rows]
        src = self.total.at[self.p.index(z, y, c), rows]
        return remote(
            src, dst, self.send.at[kind, z, h], self.recv.at[kind, z, h], device
        )

    def take(self, kind, z, y, h):
        p = self.p
        copy = self.copy(kind, z, y, p.c, h, p.sibling)
        copy.wait_recv()
        rows = pl.ds(h * self.rows, self.rows)
        if kind is None:
            term = self.from_core[y, z, rows]
        elif kind == 2:
            term = self.from_y[z, rows]
        else:
            term = self.from_z[kind, z, rows]
        return term.astype(F32)

    def add(self, kinds, z, y, h):
        rows = pl.ds(h * self.rows, self.rows)
        piece = self.p.index(z, y, self.p.c)
        value = self.total[piece, rows].astype(F32)
        for kind in kinds:
            value = value + self.take(kind, z, y, h)
        self.total[piece, rows] = value.astype(self.total.dtype)

    def core_send(self, z, y):
        for h in range(self.chunks):
            self.copy(None, z, y, 1 - self.p.c, h, self.p.sibling).start()

    def stage_y(self):
        p = self.p
        if p.Y == 1:
            return
        for k in range(p.Z - 1, -1, -1):
            for cond, z in p.by_distance(k):

                @when(cond)
                def _():
                    for h in range(self.chunks):
                        self.add([None], z, 1 - p.y, h)
                        self.copy(2, z, 1 - p.y, p.c, h, p.across).start()

    def stage_z(self):
        p = self.p
        near = [None] + ([2] if p.Y > 1 else [])
        for k in range(p.Z - 1, 0, -1):
            for h in range(self.chunks):
                for (cond, z), kind in zip(p.by_distance(k), (0, 1)):

                    @pl.when(cond)
                    def _():
                        self.add(near, z, p.y, h)
                        before = (p.has_down, p.has_up)[kind]
                        pl.when(before)(lambda: self.add([kind], z, p.y, h))
                        self.copy(kind, z, p.y, p.c, h, (p.up, p.down)[kind]).start()

            yield
        for h in range(self.chunks):
            self.add(near, p.z, p.y, h)
            pl.when(p.has_down)(lambda: self.add([0], p.z, p.y, h))
            pl.when(p.has_up)(lambda: self.add([1], p.z, p.y, h))
        yield

    def finish(self):
        p = self.p
        for z in range(p.Z):
            for h in range(self.chunks):
                pl.when(z > p.z)(lambda: self.copy(0, z, p.y, p.c, h, p.up).wait_send())
                pl.when(z < p.z)(lambda: self.copy(1, z, p.y, p.c, h, p.down).wait_send())
                if p.Y > 1:
                    self.copy(2, z, 1 - p.y, p.c, h, p.across).wait_send()
                for y in range(p.Y):
                    self.copy(None, z, y, 1 - p.c, h, p.sibling).wait_send()


def kernel(
    cfg,
    cols,
    table,
    features,
    vals,
    degree,
    w_self,
    w_neigh,
    cotangent,
    output,
    grad_features,
    grad_self,
    grad_neigh,
    everything,
    vals_t,
    dagg,
    total,
    core_in,
    y_in,
    z_in,
    w_total,
    w_core_in,
    w_y_in,
    w_z_in,
    w_all,
    g_send,
    g_recv,
    r_send,
    r_recv,
    wr_send,
    wr_recv,
    wg_send,
    wg_recv,
):
    Z, Y, chunks, per_row, factor = cfg
    p = Place(Z, Y)
    row_blocks, _, width = features.shape
    entries = vals.shape[0]
    n = 2 * Y * Z

    barrier = pltpu.get_barrier_semaphore()

    def greet(device):
        pl.semaphore_signal(
            barrier, inc=1, device_id={"rows": device}, device_id_type=pl.DeviceIdType.MESH
        )

    greet(p.sibling)
    if Y > 1:
        greet(p.across)
    pl.when(p.has_up)(lambda: greet(p.up))
    pl.when(p.has_down)(lambda: greet(p.down))
    ends = (p.z > 0).astype(jnp.int32) + (p.z < Z - 1).astype(jnp.int32)
    pl.semaphore_wait(barrier, (2 if Y > 1 else 1) + ends)

    gather = Gather(p, features, everything, chunks, g_send, g_recv)
    steps = gather.run()
    next(steps)

    for i in range(row_blocks):
        everything[p.me * row_blocks + i] = features[i]
    next(steps)

    per = entries // Z if Z <= entries else 0

    def flip(e, _):
        vals_t[e] = vals[e].T
        return 0

    for k in range(1, Z):
        if per:
            lax.fori_loop((k - 1) * per, k * per, flip, 0)
        next(steps)
    lax.fori_loop((Z - 1) * per, entries, flip, 0)
    vals_t[entries] = jnp.zeros((B, B), BF16)
    dagg[row_blocks] = jnp.zeros((B, width), BF16)
    scales = [
        jnp.broadcast_to(degree[r : r + 1, :].astype(F32), (B, B)).T for r in range(row_blocks)
    ]
    for _ in steps:
        pass

    means, dpres, owns = [], [], []
    for r in range(row_blocks):
        rows = slice(r * B, (r + 1) * B)
        left = jnp.concatenate([vals[r * per_row + j] for j in range(per_row)], axis=1)
        right = jnp.concatenate(
            [everything[cols[r * per_row + j]] for j in range(per_row)], axis=0
        )
        aggregate = jnp.dot(left, right, preferred_element_type=F32)
        mean = (aggregate / scales[r]).astype(BF16)
        own = features[r]
        pre = jnp.dot(own, w_self[...], preferred_element_type=F32) + jnp.dot(
            mean, w_neigh[...], preferred_element_type=F32
        )
        sigma = 1.0 / (1.0 + jnp.exp(-pre))
        output[rows, :] = (pre * sigma).astype(BF16)
        dpre = (cotangent[rows, :].astype(F32) * sigma * (1.0 + pre * (1.0 - sigma))).astype(BF16)
        back = lax.dot_general(dpre, w_neigh[...], NT, preferred_element_type=F32)
        dagg[r] = (back / scales[r]).astype(BF16)
        means.append(mean)
        dpres.append(dpre)
        owns.append(lax.dot_general(dpre, w_self[...], NT, preferred_element_type=F32))

    left = jnp.concatenate(
        [
            jnp.concatenate([features[r] for r in range(row_blocks)], axis=0).T,
            jnp.concatenate(means, axis=0).T,
        ],
        axis=0,
    )
    sums = jnp.dot(left, jnp.concatenate(dpres, axis=0), preferred_element_type=F32)
    w_rows = w_total.shape[1]
    for d in range(n):
        at = d * w_rows
        half, row = divmod(at, 2 * width)
        w_total[d] = sums[row : row + w_rows, half * 128 : half * 128 + 128].astype(w_total.dtype)
    w_sum = Reduce(p, w_total, w_core_in, w_y_in, w_z_in, 1, wr_send, wr_recv)
    for z in range(Z):
        for y in range(Y):
            w_sum.core_send(z, y)

    spread = Reduce(p, total, core_in, y_in, z_in, chunks, r_send, r_recv)

    def spread_piece(piece):
        for b in range(row_blocks):
            block = piece * row_blocks + b
            one, two = table[0, block], table[1, block]
            left = jnp.concatenate([vals_t[one], vals_t[two]], axis=1)
            right = jnp.concatenate([dagg[table[2, block]], dagg[table[3, block]]], axis=0)
            total[piece, b * B : (b + 1) * B] = jnp.dot(
                left, right, preferred_element_type=F32
            ).astype(BF16)

    def order(i):
        z = jnp.where(p.z < Z // 2, p.z + Z - 1 - i, p.z + 1 + i) % Z
        return z

    def for_sibling(i, _):
        y = (i % Y + p.y + 1) % Y
        z = order(i // Y)
        spread_piece(p.index(z, y, 1 - p.c))
        spread.core_send(z, y)
        return 0

    def for_own(i, _):
        spread_piece(p.index(i // Y, i % Y, p.c))
        return 0

    lax.fori_loop(0, Z * Y, for_sibling, 0)
    w_sum.stage_y()
    lax.fori_loop(0, Z * Y, for_own, 0)
    spread.stage_y()

    for _ in w_sum.stage_z():
        pass
    w_all[p.me] = w_total[p.me]
    w_gather = Gather(p, None, w_all, 1, wg_send, wg_recv)
    w_steps = w_gather.run()
    next(w_steps)
    for _ in spread.stage_z():
        next(w_steps, None)
    for r in range(row_blocks):
        rows = slice(r * B, (r + 1) * B)
        grad_features[rows, :] = (owns[r] + total[p.me, rows].astype(F32)).astype(BF16)
    for _ in w_steps:
        pass
    for d in range(n):
        at = d * w_rows
        half, row = divmod(at, 2 * width)
        target, row = ((grad_self, row), (grad_neigh, row - width))[row // width]
        target[row : row + w_rows, half * 128 : half * 128 + 128] = w_all[d].astype(F32) * factor

    gather.finish()
    w_sum.finish()
    spread.finish()
    w_gather.finish()


def body(Z, Y, features, block_cols, block_vals, degree, w_self, w_neigh, cotangent):
    nodes, width = features.shape
    hidden = w_self.shape[1]
    entries = block_cols.shape[0]
    row_blocks = nodes // B
    n = 2 * Y * Z
    blocks = n * row_blocks
    chunks = 2 if Z <= 4 else 1
    number = jnp.arange(entries, dtype=jnp.int32)[None, :]
    match = block_cols[None, :] == jnp.arange(blocks, dtype=jnp.int32)[:, None]
    first = jnp.min(jnp.where(match, number, entries), axis=1)
    last = jnp.max(jnp.where(match, number, -1), axis=1)
    last = jnp.where((last == first) | (last < 0), entries, last)
    per_row = entries // row_blocks
    table = jnp.stack([first, last, first // per_row, last // per_row])

    w_rows = 4 * width * hidden // 256 // n
    w_type = BF16 if w_rows % 16 == 0 else F32
    cfg = (Z, Y, chunks, entries // row_blocks, float(nodes * n) ** -0.5)
    vmem = pl.BlockSpec(memory_space=pltpu.VMEM)
    smem = pl.BlockSpec(memory_space=pltpu.SMEM)

    def sems(chunks):
        return [pltpu.SemaphoreType.DMA((3 + Y, Z, chunks))] * 2

    return pl.pallas_call(
        functools.partial(kernel, cfg),
        out_shape=(
            jax.ShapeDtypeStruct((nodes, hidden), BF16),
            jax.ShapeDtypeStruct((nodes, width), BF16),
            jax.ShapeDtypeStruct((width, hidden), F32),
            jax.ShapeDtypeStruct((width, hidden), F32),
        ),
        in_specs=[smem, smem] + [vmem] * 6,
        out_specs=[vmem] * 4,
        scratch_shapes=[
            pltpu.VMEM((blocks, B, width), BF16),
            pltpu.VMEM((entries + 1, B, B), BF16),
            pltpu.VMEM((row_blocks + 1, B, width), BF16),
            pltpu.VMEM((n, nodes, width), BF16),
            pltpu.VMEM((Y, Z, nodes, width), BF16),
            pltpu.VMEM((Z if Y > 1 else 1, nodes, width), BF16),
            pltpu.VMEM((2, Z, nodes, width), BF16),
            pltpu.VMEM((n, w_rows, 128), w_type),
            pltpu.VMEM((Y, Z, w_rows, 128), w_type),
            pltpu.VMEM((Z, w_rows, 128), w_type),
            pltpu.VMEM((2, Z, w_rows, 128), w_type),
            pltpu.VMEM((n, w_rows, 128), w_type),
        ]
        + sems(chunks)
        + sems(chunks)
        + sems(1)
        + sems(1),
        compiler_params=pltpu.CompilerParams(
            collective_id=0, has_side_effects=True, vmem_limit_bytes=56 * 1024 * 1024
        ),
        cost_estimate=pl.CostEstimate(
            flops=600_000_000, bytes_accessed=4_000_000, transcendentals=131072
        ),
    )(
        block_cols,
        table,
        features.reshape(row_blocks, B, width),
        block_vals,
        degree.reshape(row_blocks, B),
        w_self,
        w_neigh,
        cotangent,
    )


def solution(mesh):
    rows = mesh.shape["rows"]
    Y = 2 if rows <= 16 and rows % 4 == 0 else 1
    Z = rows // (2 * Y)
    return jax.shard_map(
        functools.partial(body, Z, Y),
        mesh=mesh,
        in_specs=(
            P(("groups", "rows"), None),
            P(("groups", "rows")),
            P(("groups", "rows"), None, None),
            P(("groups", "rows")),
            P(),
            P(),
            P(("groups", "rows"), None),
        ),
        out_specs=(
            P(("groups", "rows"), None),
            P(("groups", "rows"), None),
            P("groups", None),
            P("groups", None),
        ),
        check_vma=False,
    )
```

time: 235 us -> 59.8 us (0.25)
  waiting for transfers between devices: 194 us -> 0 us
  Pallas kernels: 0 us -> 53.2 us
  between operations: 13.9 us -> 0.66 us
  matrix products: 8.79 us -> 0 us
  other arithmetic: 8.71 us -> 0.69 us
  local copies, waits for them, and re-layouts: 8.74 us -> 4.91 us
    psum x1 -> x0, waiting for transfers between devices: 75.2 us -> none  [body(): lax.psum((jnp.dot(features.T, dpre, preferred_element_type=jnp.float32),...]
    reduce_scatter x1 -> x0, waiting for transfers between devices: 74.6 us -> none  [body(): lax.psum_scatter(total.reshape(count, width), 'rows', scatter_dimension=0...]
    pallas_call x0 -> x1, Pallas kernels: none -> 53.2 us  [body(): pl.pallas_call(functools.partial(kernel, cfg), out_shape=(jax.ShapeDtypeS...]
    all_gather x1 -> x0, waiting for transfers between devices: 43.9 us -> none  [body(): everything = lax.all_gather(features, 'rows', axis=0, tiled=True)]
    dot_general x8 -> x0, matrix products: 8.79 us -> none  [the longest x1 1.84 us: body(): jnp.dot(dpre, w_self.T, preferred_element_type=jnp.float32) + spread]
    scatter-add x1 -> x0, other arithmetic: 6.23 us -> none  [body(): jnp.zeros((number, 128, width), jnp.float32).at[target]]
    unnamed x12, local copies, waits for them, and re-layouts: 1.54 us -> 4.91 us
    broadcast_in_dim x2 -> x0, local copies, waits for them, and re-layouts: 2.68 us -> none  [the longest x1 2.46 us: body(): jnp.zeros((number, 128, width), jnp.float32).at[target]]
  transfers between devices with their start and end apart: 3 -> 0, of which waited for: 3 -> 0; matrix products, arithmetic and copies ran while one was open for 7% -> 0% of each run, Pallas kernels for 0% -> 0%
where the time goes in v1:
time: 59.8 us; the launch traced here: 59.5 us
  Pallas kernels  53.2 us (89%)
  local copies, waits for them, and re-layouts  4.91 us (8%)
  other arithmetic  0.69 us (1%)
  between operations  0.66 us (1%)
    pallas_call x1, Pallas kernels, body(): pl.pallas_call(functools.partial(kernel, cfg), out_shape=(jax.ShapeDtypeS...  53.2 us
    unnamed x12, local copies, waits for them, and re-layouts  4.91 us

profile of v1, /device:TPU:0, one launch (start us, length us, event | category | flops | bytes accessed | tf_op | source)
XLA Modules:
  0.0 59.5 jit_solution(9082358363374785775)
XLA Ops:
  0.6 0.0 copy-start.3
  0.6 0.6 %copy-done.3 = s32[32]{0:T(128)S(1)} copy-done((s32[32]{0:T(128)S(1)}, s32[32]{0:T(128)}, u32[]{:S(2)}) %copy-start.3) | copy-done | bytes 152
  1.3 0.1 select_reduce_fusion.1
  1.4 0.6 pad_add_fusion.table
  2.0 53.2 %shard_map.102 = (bf16[512,256]{1,0:T(8,128)(2,1)}, bf16[512,128]{1,0:T(8,128)(2,1)}, f32[128,256]{1,0:T(8,128)}, f32[128,256]{1,0:T(8,128)}) custom-call(s32[32]{0:T(128)} %cols.1, s32[4,64]{1,0:T(4,128)} %pad_add_fusion.table, bf16[4,128,128]{2,1,0:T(8,128)(2,1)} %bitcast.10, bf16[32,128,128]{2,1,0:T(8,128)(2,1)} %vals.1, s32[4,128]{1,0:T(4,128)} %bitcast.11, ...), custom_call_target="tpu_custom_call" | custom-call | flops 600000000 | bytes 4000000 | tf_op jit(solution)/shard_map/pallas_call | solution.py:450
  55.2 0.0 copy-start.2
  55.2 1.7 %copy.15 = bf16[512,256]{1,0:T(8,128)(2,1)} copy(bf16[512,256]{1,0:T(8,128)(2,1)} %get-tuple-element.13) | data formatting | bytes 524288
  56.9 0.0 copy-done.2
  56.9 0.0 copy-start.1
  56.9 0.7 %copy.16 = bf16[512,128]{1,0:T(8,128)(2,1)} copy(bf16[512,128]{1,0:T(8,128)(2,1)S(1)} %copy-done.2) | data formatting | bytes 262144
  57.6 0.3 copy-done.1
  57.9 0.0 copy-start
  57.9 0.7 %copy.17 = f32[128,256]{1,0:T(8,128)} copy(f32[128,256]{1,0:T(8,128)S(1)} %copy-done.1) | data formatting | bytes 262144
  58.6 0.3 copy-done
  58.8 0.7 %copy.18 = f32[128,256]{1,0:T(8,128)} copy(f32[128,256]{1,0:T(8,128)S(1)} %copy-done) | data formatting | bytes 262144
  (1 shorter events, 0.0 us)
Async XLA Ops:
  0.6 0.7 %copy-start.3 = (s32[32]{0:T(128)S(1)}, s32[32]{0:T(128)}, u32[]{:S(2)}) copy-start(s32[32]{0:T(128)} %cols.1) | copy-start | bytes 388
  55.2 1.7 %copy-start.2 = (bf16[512,128]{1,0:T(8,128)(2,1)S(1)}, bf16[512,128]{1,0:T(8,128)(2,1)}, u32[]{:S(2)}) copy-start(bf16[512,128]{1,0:T(8,128)(2,1)} %get-tuple-element.14) | copy-start | bytes 393220
  56.9 1.0 %copy-start.1 = (f32[128,256]{1,0:T(8,128)S(1)}, f32[128,256]{1,0:T(8,128)}, u32[]{:S(2)}) copy-start(f32[128,256]{1,0:T(8,128)} %get-tuple-element.15) | copy-start | bytes 393220
  57.9 1.0 %copy-start = (f32[128,256]{1,0:T(8,128)S(1)}, f32[128,256]{1,0:T(8,128)}, u32[]{:S(2)}) copy-start(f32[128,256]{1,0:T(8,128)} %get-tuple-element.16) | copy-start | bytes 393220

commit v2 on v1

--- a/solution.py
+++ b/solution.py
@@ -247,12 +247,12 @@
     cols,
     table,
     features,
-    vals,
+    vals_hbm,
     degree,
     w_self,
     w_neigh,
-    cotangent,
-    output,
+    cotangent_hbm,
+    output_hbm,
     grad_features,
     grad_self,
     grad_neigh,
@@ -276,11 +276,20 @@
     wr_recv,
     wg_send,
     wg_recv,
+    vals,
+    cotangent,
+    output,
+    local,
 ):
     Z, Y, chunks, per_row, factor = cfg
     p = Place(Z, Y)
     row_blocks, _, width = features.shape
     entries = vals.shape[0]
+    vals_in = pltpu.make_async_copy(vals_hbm, vals, local.at[0])
+    cotangent_in = pltpu.make_async_copy(cotangent_hbm, cotangent, local.at[1])
+    output_out = pltpu.make_async_copy(output, output_hbm, local.at[2])
+    vals_in.start()
+    cotangent_in.start()
     n = 2 * Y * Z
 
     barrier = pltpu.get_barrier_semaphore()
@@ -304,6 +313,8 @@
 
     for i in range(row_blocks):
         everything[p.me * row_blocks + i] = features[i]
+    vals_in.wait()
+    cotangent_in.wait()
     next(steps)
 
     per = entries // Z if Z <= entries else 0
@@ -347,6 +358,8 @@
         dpres.append(dpre)
         owns.append(lax.dot_general(dpre, w_self[...], NT, preferred_element_type=F32))
 
+    output_out.start()
+
     left = jnp.concatenate(
         [
             jnp.concatenate([features[r] for r in range(row_blocks)], axis=0).T,
@@ -397,29 +410,56 @@
     lax.fori_loop(0, Z * Y, for_own, 0)
     spread.stage_y()
 
-    for _ in w_sum.stage_z():
+    w_steps, t_steps = w_sum.stage_z(), spread.stage_z()
+    next(w_steps)
+    next(t_steps)
+    for _ in w_steps:
         pass
     w_all[p.me] = w_total[p.me]
-    w_gather = Gather(p, None, w_all, 1, wg_send, wg_recv)
-    w_steps = w_gather.run()
-    next(w_steps)
-    for _ in spread.stage_z():
-        next(w_steps, None)
+
+    def hand(i, source):
+        mine = w_all.at[source]
+        return remote(mine, mine, wg_send.at[i], wg_recv.at[i], (p.me + i) % n)
+
+    def hand_start(i, _):
+        hand(i, p.me).start()
+        return 0
+
+    def hand_wait(i, _):
+        hand(i, (p.me + n - i) % n).wait_recv()
+        return 0
+
+    def hand_finish(i, _):
+        hand(i, p.me).wait_send()
+        return 0
+
+    lax.fori_loop(1, n, hand_start, 0)
+    for _ in t_steps:
+        pass
     for r in range(row_blocks):
         rows = slice(r * B, (r + 1) * B)
         grad_features[rows, :] = (owns[r] + total[p.me, rows].astype(F32)).astype(BF16)
-    for _ in w_steps:
-        pass
+    lax.fori_loop(1, n, hand_wait, 0)
     for d in range(n):
         at = d * w_rows
         half, row = divmod(at, 2 * width)
         target, row = ((grad_self, row), (grad_neigh, row - width))[row // width]
         target[row : row + w_rows, half * 128 : half * 128 + 128] = w_all[d].astype(F32) * factor
 
+    output_out.wait()
     gather.finish()
     w_sum.finish()
     spread.finish()
-    w_gather.finish()
+    lax.fori_loop(1, n, hand_finish, 0)
+
+
+def hand_over(a, b, c, d, a_out, b_out, c_out, d_out, sems):
+    pairs = ((a, a_out), (b, b_out), (c, c_out), (d, d_out))
+    copies = [pltpu.make_async_copy(x, y, sems.at[i]) for i, (x, y) in enumerate(pairs)]
+    for copy in copies:
+        copy.start()
+    for copy in copies:
+        copy.wait()
 
 
 def body(Z, Y, features, block_cols, block_vals, degree, w_self, w_neigh, cotangent):
@@ -443,11 +483,12 @@
     cfg = (Z, Y, chunks, entries // row_blocks, float(nodes * n) ** -0.5)
     vmem = pl.BlockSpec(memory_space=pltpu.VMEM)
     smem = pl.BlockSpec(memory_space=pltpu.SMEM)
+    hbm = pl.BlockSpec(memory_space=pl.ANY)
 
     def sems(chunks):
         return [pltpu.SemaphoreType.DMA((3 + Y, Z, chunks))] * 2
 
-    return pl.pallas_call(
+    results = pl.pallas_call(
         functools.partial(kernel, cfg),
         out_shape=(
             jax.ShapeDtypeStruct((nodes, hidden), BF16),
@@ -455,8 +496,8 @@
             jax.ShapeDtypeStruct((width, hidden), F32),
             jax.ShapeDtypeStruct((width, hidden), F32),
         ),
-        in_specs=[smem, smem] + [vmem] * 6,
-        out_specs=[vmem] * 4,
+        in_specs=[smem, smem, vmem, hbm, vmem, vmem, vmem, hbm],
+        out_specs=[hbm, vmem, vmem, vmem],
         scratch_shapes=[
             pltpu.VMEM((blocks, B, width), BF16),
             pltpu.VMEM((entries + 1, B, B), BF16),
@@ -474,7 +515,13 @@
         + sems(chunks)
         + sems(chunks)
         + sems(1)
-        + sems(1),
+        + [pltpu.SemaphoreType.DMA((n,))] * 2
+        + [
+            pltpu.VMEM((entries, B, B), BF16),
+            pltpu.VMEM((nodes, hidden), BF16),
+            pltpu.VMEM((nodes, hidden), BF16),
+            pltpu.SemaphoreType.DMA((3,)),
+        ],
         compiler_params=pltpu.CompilerParams(
             collective_id=0, has_side_effects=True, vmem_limit_bytes=56 * 1024 * 1024
         ),
@@ -491,6 +538,14 @@
         w_neigh,
         cotangent,
     )
+    anywhere = pl.BlockSpec(memory_space=pl.ANY)
+    return pl.pallas_call(
+        hand_over,
+        out_shape=tuple(jax.ShapeDtypeStruct(x.shape, x.dtype) for x in results),
+        in_specs=[pl.BlockSpec(memory_space=pltpu.VMEM)] * 4,
+        out_specs=[anywhere] * 4,
+        scratch_shapes=[pltpu.SemaphoreType.DMA((4,))],
+    )(*results)
 
 
 def solution(mesh):

time: 59.8 us -> 55.8 us (0.933)
  local copies, waits for them, and re-layouts: 4.91 us -> 0.65 us
    unnamed x12 -> x2, local copies, waits for them, and re-layouts: 4.91 us -> 0.65 us
    pallas_call x0 -> x1, Pallas kernels: none -> 1.98 us  [body(): pl.pallas_call(hand_over, out_shape=tuple((jax.ShapeDtypeStruct(x.shape,...]
    pallas_call x1, Pallas kernels: 53.2 us -> 51.6 us  [body(): pl.pallas_call(functools.partial(kernel, cfg), out_shape=(jax.ShapeDtypeS...]
where the time goes in v2:
time: 55.8 us; the launch traced here: 55.6 us
  Pallas kernels  53.6 us (96%)
  other arithmetic  0.69 us (1%)
  local copies, waits for them, and re-layouts  0.65 us (1%)
  between operations  0.65 us (1%)
    pallas_call x1, Pallas kernels, body(): pl.pallas_call(functools.partial(kernel, cfg), out_shape=(jax.ShapeDtypeS...  51.6 us
    pallas_call x1, Pallas kernels, body(): pl.pallas_call(hand_over, out_shape=tuple((jax.ShapeDtypeStruct(x.shape,...  1.98 us

profile of v2, /device:TPU:0, one launch (start us, length us, event | category | flops | bytes accessed | tf_op | source)
XLA Modules:
  0.0 55.6 jit_solution(7803575692740492470)
XLA Ops:
  0.6 0.0 copy-start
  0.6 0.6 %copy-done = s32[32]{0:T(128)S(1)} copy-done((s32[32]{0:T(128)S(1)}, s32[32]{0:T(128)}, u32[]{:S(2)}) %copy-start) | copy-done | bytes 152
  1.3 0.1 select_reduce_fusion.1
  1.4 0.6 %pad_add_fusion.table = s32[4,64]{1,0:T(4,128)} fusion(s32[1,64]{1,0:T(1,128)S(1)} %get-tuple-element.14, s32[1,64]{1,0:T(1,128)S(1)} %get-tuple-element.16, s32[1,64]{1,0:T(1,128)S(1)} %get-tuple-element.15, s32[1,64]{1,0:T(1,128)S(1)} %bitcast.9), kind=kLoop, calls=%fused_computation.3 | loop fusion | flops 768 | bytes 2048 | tf_op jit(solution)/shard_map/stack | solution.py:479
  2.0 51.6 %shard_map.102 = (bf16[512,256]{1,0:T(8,128)(2,1)}, bf16[512,128]{1,0:T(8,128)(2,1)}, f32[128,256]{1,0:T(8,128)}, f32[128,256]{1,0:T(8,128)}) custom-call(s32[32]{0:T(128)} %cols.1, s32[4,64]{1,0:T(4,128)} %pad_add_fusion.table, bf16[4,128,128]{2,1,0:T(8,128)(2,1)} %bitcast.10, bf16[32,128,128]{2,1,0:T(8,128)(2,1)} %vals_hbm.1, s32[4,128]{1,0:T(4,128)} %bitcast.11, ...), custom_call_target="tpu_custom_call" | custom-call | flops 600000000 | bytes 4000000 | tf_op jit(solution)/shard_map/pallas_call | solution.py:491
  53.6 2.0 %shard_map.103 = (bf16[512,256]{1,0:T(8,128)(2,1)}, bf16[512,128]{1,0:T(8,128)(2,1)}, f32[128,256]{1,0:T(8,128)}, f32[128,256]{1,0:T(8,128)}) custom-call(bf16[512,256]{1,0:T(8,128)(2,1)} %get-tuple-element.8.a, bf16[512,128]{1,0:T(8,128)(2,1)} %get-tuple-element.9.b, f32[128,256]{1,0:T(8,128)} %get-tuple-element.10.c, f32[128,256]{1,0:T(8,128)} %get-tuple-element.11.d), custom_call_target="tpu_custom_call" | custom-call | tf_op jit(solution)/shard_map/pallas_call | solution.py:542
  (1 shorter events, 0.0 us)
Async XLA Ops:
  0.6 0.7 %copy-start = (s32[32]{0:T(128)S(1)}, s32[32]{0:T(128)}, u32[]{:S(2)}) copy-start(s32[32]{0:T(128)} %cols.1) | copy-start | bytes 388

commit v3 on v2

--- a/solution.py
+++ b/solution.py
@@ -368,15 +368,59 @@
         axis=0,
     )
     sums = jnp.dot(left, jnp.concatenate(dpres, axis=0), preferred_element_type=F32)
-    w_rows = w_total.shape[1]
+    w_rows = w_total.shape[3]
     for d in range(n):
         at = d * w_rows
         half, row = divmod(at, 2 * width)
-        w_total[d] = sums[row : row + w_rows, half * 128 : half * 128 + 128].astype(w_total.dtype)
-    w_sum = Reduce(p, w_total, w_core_in, w_y_in, w_z_in, 1, wr_send, wr_recv)
-    for z in range(Z):
-        for y in range(Y):
-            w_sum.core_send(z, y)
+        w_total[d % 2, d // 2 % Y, d // 2 // Y] = sums[row : row + w_rows, half * 128 : half * 128 + 128].astype(w_total.dtype)
+    w_type = w_total.dtype
+    w_core = remote(
+        w_total.at[1 - p.c], w_core_in, wr_send.at[3, 0, 0], wr_recv.at[3, 0, 0], p.sibling
+    )
+    w_y = remote(
+        w_total.at[p.c, (p.y + 1) % Y], w_y_in, wr_send.at[2, 0, 0], wr_recv.at[2, 0, 0], p.across
+    )
+
+    def w_z(kind, z):
+        return remote(
+            w_total.at[p.c, p.y, z],
+            w_z_in.at[kind, z],
+            wr_send.at[kind, z, 0],
+            wr_recv.at[kind, z, 0],
+            (p.up, p.down)[kind],
+        )
+
+    def w_add(kind, z):
+        remote(
+            w_z_in.at[kind, z],
+            w_z_in.at[kind, z],
+            wr_send.at[kind, z, 0],
+            wr_recv.at[kind, z, 0],
+            p.sibling,
+        ).wait_recv()
+        value = w_total[p.c, p.y, z].astype(F32) + w_z_in[kind, z].astype(F32)
+        w_total[p.c, p.y, z] = value.astype(w_type)
+
+    def w_stage_z():
+        if Y > 1:
+            w_y.wait_recv()
+            value = w_total[p.c, p.y].astype(F32) + w_y_in[...].astype(F32)
+            w_total[p.c, p.y] = value.astype(w_type)
+        for k in range(Z - 1, 0, -1):
+            for (cond, z), kind in zip(p.by_distance(k), (0, 1)):
+
+                @pl.when(cond)
+                def _():
+                    before = (p.has_down, p.has_up)[kind]
+                    pl.when(before)(lambda: w_add(kind, z))
+                    w_z(kind, z).start()
+
+            yield
+        pl.when(p.has_down)(lambda: w_add(0, p.z))
+        pl.when(p.has_up)(lambda: w_add(1, p.z))
+        yield
+
+    w_core.start()
 
     spread = Reduce(p, total, core_in, y_in, z_in, chunks, r_send, r_recv)
 
@@ -406,16 +450,19 @@
         return 0
 
     lax.fori_loop(0, Z * Y, for_sibling, 0)
-    w_sum.stage_y()
+    w_core.wait_recv()
+    w_total[p.c] = (w_total[p.c].astype(F32) + w_core_in[...].astype(F32)).astype(w_type)
+    if Y > 1:
+        w_y.start()
     lax.fori_loop(0, Z * Y, for_own, 0)
     spread.stage_y()
 
-    w_steps, t_steps = w_sum.stage_z(), spread.stage_z()
+    w_steps, t_steps = w_stage_z(), spread.stage_z()
     next(w_steps)
     next(t_steps)
     for _ in w_steps:
         pass
-    w_all[p.me] = w_total[p.me]
+    w_all[p.me] = w_total[p.c, p.y, p.z]
 
     def hand(i, source):
         mine = w_all.at[source]
@@ -448,7 +495,12 @@
 
     output_out.wait()
     gather.finish()
-    w_sum.finish()
+    w_core.wait_send()
+    if Y > 1:
+        w_y.wait_send()
+    for z in range(Z):
+        pl.when(z > p.z)(lambda: w_z(0, z).wait_send())
+        pl.when(z < p.z)(lambda: w_z(1, z).wait_send())
     spread.finish()
     lax.fori_loop(1, n, hand_finish, 0)
 
@@ -506,7 +558,7 @@
             pltpu.VMEM((Y, Z, nodes, width), BF16),
             pltpu.VMEM((Z if Y > 1 else 1, nodes, width), BF16),
             pltpu.VMEM((2, Z, nodes, width), BF16),
-            pltpu.VMEM((n, w_rows, 128), w_type),
+            pltpu.VMEM((2, Y, Z, w_rows, 128), w_type),
             pltpu.VMEM((Y, Z, w_rows, 128), w_type),
             pltpu.VMEM((Z, w_rows, 128), w_type),
             pltpu.VMEM((2, Z, w_rows, 128), w_type),

time: 55.8 us -> 55.6 us (level)
  no operation moved by 1% of the time
where the time goes in v3:
time: 55.6 us; the launch traced here: 55.4 us
  Pallas kernels  53.5 us (96%)
  other arithmetic  0.69 us (1%)
  local copies, waits for them, and re-layouts  0.65 us (1%)
  between operations  0.65 us (1%)
    pallas_call x1, Pallas kernels, body(): pl.pallas_call(functools.partial(kernel, cfg), out_shape=(jax.ShapeDtypeS...  51.5 us
    pallas_call x1, Pallas kernels, body(): pl.pallas_call(hand_over, out_shape=tuple((jax.ShapeDtypeStruct(x.shape,...  1.98 us

profile of v3, /device:TPU:0, one launch (start us, length us, event | category | flops | bytes accessed | tf_op | source)
XLA Modules:
  0.0 55.4 jit_solution(6394729471457751725)
XLA Ops:
  0.6 0.0 copy-start
  0.6 0.6 %copy-done = s32[32]{0:T(128)S(1)} copy-done((s32[32]{0:T(128)S(1)}, s32[32]{0:T(128)}, u32[]{:S(2)}) %copy-start) | copy-done | bytes 152
  1.3 0.1 select_reduce_fusion.1
  1.4 0.6 %pad_add_fusion.table = s32[4,64]{1,0:T(4,128)} fusion(s32[1,64]{1,0:T(1,128)S(1)} %get-tuple-element.14, s32[1,64]{1,0:T(1,128)S(1)} %get-tuple-element.16, s32[1,64]{1,0:T(1,128)S(1)} %get-tuple-element.15, s32[1,64]{1,0:T(1,128)S(1)} %bitcast.9), kind=kLoop, calls=%fused_computation.3 | loop fusion | flops 768 | bytes 2048 | tf_op jit(solution)/shard_map/stack | solution.py:531
  2.0 51.5 %shard_map.102 = (bf16[512,256]{1,0:T(8,128)(2,1)}, bf16[512,128]{1,0:T(8,128)(2,1)}, f32[128,256]{1,0:T(8,128)}, f32[128,256]{1,0:T(8,128)}) custom-call(s32[32]{0:T(128)} %cols.1, s32[4,64]{1,0:T(4,128)} %pad_add_fusion.table, bf16[4,128,128]{2,1,0:T(8,128)(2,1)} %bitcast.10, bf16[32,128,128]{2,1,0:T(8,128)(2,1)} %vals_hbm.1, s32[4,128]{1,0:T(4,128)} %bitcast.11, ...), custom_call_target="tpu_custom_call" | custom-call | flops 600000000 | bytes 4000000 | tf_op jit(solution)/shard_map/pallas_call | solution.py:543
  53.5 2.0 %shard_map.103 = (bf16[512,256]{1,0:T(8,128)(2,1)}, bf16[512,128]{1,0:T(8,128)(2,1)}, f32[128,256]{1,0:T(8,128)}, f32[128,256]{1,0:T(8,128)}) custom-call(bf16[512,256]{1,0:T(8,128)(2,1)} %get-tuple-element.8.a, bf16[512,128]{1,0:T(8,128)(2,1)} %get-tuple-element.9.b, f32[128,256]{1,0:T(8,128)} %get-tuple-element.10.c, f32[128,256]{1,0:T(8,128)} %get-tuple-element.11.d), custom_call_target="tpu_custom_call" | custom-call | tf_op jit(solution)/shard_map/pallas_call | solution.py:594
  (1 shorter events, 0.0 us)
Async XLA Ops:
  0.6 0.7 %copy-start = (s32[32]{0:T(128)S(1)}, s32[32]{0:T(128)}, u32[]{:S(2)}) copy-start(s32[32]{0:T(128)} %cols.1) | copy-start | bytes 388
